TPU v7x, 32 devices: a whole 2x2x4 slice. The times are simulated.
32 devices in a mesh: run: 2 (over y), lon: 4 (over z), node: 2 (over x), lev: 2 (over core).
Axes of the slice: x: 2, y: 2, z: 4, core: 2. Of those that a mesh axis runs over, the one named last changes fastest.
Arguments:
- initial_state: float32 [8, 4, 96, 512], P(None, 'lev', 'run', 'lon'), parts along dimension 2, may hold values from -6 to 6
- node_states: float32 [8, 8, 4, 96, 512], P('node', None, 'lev', 'run', 'lon'), parts along dimension 3, may hold values from -6 to 6
- node_order: int32 [8], replicated, may hold values from 0 to 7, each once
- sector_depth: int32 [8, 96], P('node', 'run'), parts along dimension 1, may hold values from 0 to 2, as said below
- cell_offset: int32 [8, 96], P('node', 'run'), parts along dimension 1, may hold values from 2 to 127
- fraction: float32 [8, 96], P('node', 'run'), parts along dimension 1, may hold values from 0 to 1
- reaction_matrix: float32 [8, 8], replicated, may hold values from -2 to 2
- diffusivity: float32 [4], P('lev'), may hold values from 0.1 to 1
Outputs:
- new_states: float32 [8, 8, 4, 96, 512], P('node', None, 'lev', 'run', 'lon'), parts along dimension 3
There are 2 independent parts, one for each index of `run`. A program takes and returns all parts, laid end to end along the dimension named above; an argument that names none is the same for every part. Nothing has to cross between parts.
Inputs may be any that keep to these rules, and one draw needn't show every extreme that they name: `sector_depth`: rows among the 6 nearest either pole have depth 2 or more, all other rows depth 0 or 1; the rows at both poles have depth 2, the middle row depth 0.
All inputs are finite; a program needn't handle non-finite values.
Results may differ from a plain program's by a relative error of at most 0.0003.
Values sent between devices are 32-bit elements; how exact they have to be, the bound alone decides.
A program may use at most 128 MiB of HBM per device.

v0:
```python
import jax
import jax.numpy as jnp
import numpy as np
from jax import lax
from jax.sharding import PartitionSpec as P

NODES = 8
time_step = 0.5
lobatto_points = [
    -1.0,
    -0.8717401485096066,
    -0.5917001814331423,
    -0.2092992179024789,
    0.2092992179024789,
    0.5917001814331423,
    0.8717401485096066,
    1.0,
]


def padded_2(array, sides, width):
    for axis, dim in sides:
        size, length = (lax.axis_size(axis), array.shape[dim])
        up = [(i, (i + 1) % size) for i in range(size - 1)]
        down = [(j, i) for i, j in up]
        last = lax.slice_in_dim(array, length - width, length, axis=dim)
        first = lax.slice_in_dim(array, 0, width, axis=dim)
        before = lax.ppermute(last, axis, up)
        after = lax.ppermute(first, axis, down)
        array = jnp.concatenate([before, array, after], axis=dim)
    return array


def passed_along(array, axis, by):
    length = lax.axis_size(axis)
    return lax.ppermute(array, axis, [(i, (i + by) % length) for i in range(length)])


def lobatto_table():
    points = [(value + 1.0) / 2.0 for value in lobatto_points]
    result_rows = [[0.0] * 8 for m in range(8)]
    for j in range(8):
        poly_coeffs = [1.0]
        for k in range(8):
            if k != j:
                factor = 1.0 / (points[j] - points[k])
                grown = [0.0] * (len(poly_coeffs) + 1)
                for i in range(len(poly_coeffs)):
                    grown[i + 1] = grown[i + 1] + poly_coeffs[i] * factor
                    grown[i] = grown[i] - poly_coeffs[i] * points[k] * factor
                poly_coeffs = grown
        for m in range(8):
            total_value = 0.0
            for i in range(len(poly_coeffs)):
                total_value = total_value + poly_coeffs[i] * points[m] ** (i + 1) / (i + 1)
            result_rows[m][j] = total_value
    return np.array(result_rows)


def cubic_weights(fraction):
    return (
        -fraction * (fraction - 1.0) * (fraction - 2.0) / 6.0,
        (fraction + 1.0) * (fraction - 1.0) * (fraction - 2.0) / 2.0,
        -(fraction + 1.0) * fraction * (fraction - 2.0) / 2.0,
        (fraction + 1.0) * fraction * (fraction - 1.0) / 6.0,
    )


def section_matrix(node_order):
    onehot = (node_order[:, None] == jnp.arange(NODES, dtype=jnp.int32)[None, :]).astype(
        jnp.float32
    )
    quad_values = jnp.asarray(lobatto_table(), jnp.float32)
    left = jnp.dot(onehot, quad_values, precision=lax.Precision.HIGHEST)
    return jnp.dot(left, onehot.T, precision=lax.Precision.HIGHEST)


def tendency_of(states, reaction_matrix, diffusivity):
    level_count = states.shape[2]
    padded = padded_2(states, (("lev", 2),), 1)
    level_pos = lax.axis_index("lev")
    level_last = lax.axis_size("lev") - 1
    below = padded[:, :, :level_count]
    above = padded[:, :, 2:]
    bottom_level = jnp.where(level_pos == 0, states[:, :, :1], below[:, :, :1])
    below = jnp.concatenate([bottom_level, below[:, :, 1:]], axis=2)
    top_level = jnp.where(
        level_pos == level_last, states[:, :, level_count - 1 :], above[:, :, level_count - 1 :]
    )
    above = jnp.concatenate([above[:, :, : level_count - 1], top_level], axis=2)
    curvature = above - 2.0 * states + below
    reaction = jnp.einsum(
        "ts,mslyx->mtlyx", reaction_matrix, jnp.tanh(states), precision=lax.Precision.HIGHEST
    )
    return reaction + diffusivity[None, None, :, None, None] * curvature


def cut_window(field, start, length):
    return lax.dynamic_slice_in_dim(field, start, length, 2)


def advect_rows(sectioned, sector_depth, cell_offset, fraction):
    sector_cells = sectioned.shape[4]
    reach_max = min(4, lax.axis_size("lon") - 2) + 1
    depth_cells = sector_depth[:, None, None, :, None]
    nearer = jnp.where(depth_cells == 0, sectioned, 0.0)
    farther = jnp.zeros_like(sectioned)
    previous = sectioned
    for distance in range(1, reach_max + 1):
        source = previous
        arrived = passed_along(source, "lon", 1)
        previous = arrived
        nearer = nearer + jnp.where(depth_cells == distance, arrived, 0.0)
        farther = farther + jnp.where(depth_cells + 1 == distance, arrived, 0.0)
    window = jnp.concatenate([farther, nearer], axis=4)
    starts = sector_cells - cell_offset - 1
    cut_len = sector_cells + 3
    per_row = jax.vmap(cut_window, in_axes=(2, 0, None), out_axes=2)
    per_slot = jax.vmap(per_row, in_axes=(0, 0, None), out_axes=0)
    pieces = per_slot(window, starts, cut_len)
    coeffs = cubic_weights(fraction)
    result = jnp.zeros_like(sectioned)
    for stencil in range(4):
        result = (
            result
            + coeffs[stencil][:, None, None, :, None]
            * pieces[:, :, :, :, stencil : stencil + sector_cells]
        )
    return result


def shards(
    initial_state,
    node_states,
    node_order,
    sector_depth,
    cell_offset,
    fraction,
    reaction_matrix,
    diffusivity,
):
    slots = node_states.shape[0]
    weights = section_matrix(node_order)
    node_pos = lax.axis_index("node")
    tendency = tendency_of(node_states, reaction_matrix, diffusivity)
    own_rows = lax.dynamic_slice_in_dim(weights, node_pos * slots, slots, 0)
    integral = jnp.einsum(
        "mj,jtlyx->mtlyx",
        own_rows,
        lax.all_gather(tendency, "node", axis=0, tiled=True),
        precision=lax.Precision.HIGHEST,
    )
    sectioned = initial_state[None] + time_step * integral
    return advect_rows(sectioned, sector_depth, cell_offset, fraction)


def solution(mesh):
    in_specs = (
        P(None, "lev", "run", "lon"),
        P("node", None, "lev", "run", "lon"),
        P(),
        P("node", "run"),
        P("node", "run"),
        P("node", "run"),
        P(),
        P("lev"),
    )
    out_specs = P("node", None, "lev", "run", "lon")
    return jax.shard_map(shards, mesh=mesh, in_specs=in_specs, out_specs=out_specs, check_vma=False)
```

profile of v0, /device:TPU:0, one launch (start us, length us, event | category | flops | bytes accessed | tf_op | source)
XLA Modules:
  0.0 328.9 jit_solution(18254070785637578791)
XLA Ops:
  6.5 0.0 copy-start
  6.5 0.0 all-gather.2.cloned.1.call-start
  6.5 2.8 fusion.31
  9.3 1.3 collective-permute-start
  10.6 4.8 %collective-permute-start.1 = (f32[4,8,1,48,128]{4,3,2,1,0:T(8,128)}, f32[4,8,1,48,128]{4,3,2,1,0:T(8,128)}, u32[]{:S(2)}, u32[]{:S(2)}) collective-permute-start(f32[4,8,1,48,128]{4,3,2,1,0:T(8,128)} %get-tuple-element.9), channel_id=1, source_target_pairs={{0,1},{2,3},{4,5},{6,7},{8,9},{10,11},{12,13},{14,15},{16,17},{18,... | collective-permute-start | bytes 2359304 | tf_op jit(solution)/shard_map/ppermute | solution.py:28
  15.4 0.0 copy-done.2
  15.4 0.2 tanh.3
  15.6 0.0 copy-done
  15.6 2.4 fusion.8
  18.1 0.0 copy-start.7
  18.1 0.0 collective-permute-done
  18.1 0.0 collective-permute-done.1
  18.1 1.4 broadcast_select_fusion
  19.5 0.0 copy-done.7
  19.5 3.2 fusion.7
  22.7 0.0 all-gather.2.cloned.1.call-update
  22.7 0.6 copy-done.8
  23.4 0.0 copy-done.9
  23.4 0.2 fusion.14
  23.6 0.2 fusion.13
  23.8 0.0 copy-start.4
  23.8 46.7 %all-gather.2.cloned.1.call-done = f32[8,8,2,48,128]{4,3,2,1,0:T(8,128)} async-done(((f32[4,8,2,48,128]{4,3,2,1,0:T(8,128)}), f32[8,8,2,48,128]{4,3,2,1,0:T(8,128)}) %all-gather.2.cloned.1.call-update) | async-done | bytes 3145744 | tf_op jit(solution)/shard_map/all_gather | solution.py:150
  70.5 0.0 copy-done.3
  70.5 6.5 %multiply_add_fusion = f32[4,8,2,48,128]{4,0,3,2,1:T(4,128)S(1)} fusion(f32[8,8,2,48,128]{4,3,2,1,0:T(8,128)} %all-gather.2.cloned.1.call-done, f32[8,2,48,128]{3,2,1,0:T(8,128)S(1)} %copy-done.3, f32[8,8]{1,0:T(8,128)S(1)} %fusion.13, s32[]{:T(128)S(6)} %select_n.42), kind=kOutput, calls=%fused_computation.19 | convolution fusion | flops 38535168 | bytes 5113860 | tf_op jit(solution)/shard_map/mj,jtlyx->mtlyx/dot_general | solution.py:147
  77.0 1.5 collective-permute-start.2
  78.6 36.4 %collective-permute-done.2 = f32[4,8,2,48,128]{4,0,3,2,1:T(4,128)S(1)} collective-permute-done((f32[4,8,2,48,128]{4,0,3,2,1:T(4,128)S(1)}, f32[4,8,2,48,128]{4,0,3,2,1:T(4,128)S(1)}, u32[]{:S(2)}, u32[]{:S(2)}) %collective-permute-start.2) | collective-permute-done | bytes 1572896 | tf_op jit(solution)/shard_map/ppermute | solution.py:36
  115.0 0.0 collective-permute-start.3
  115.0 37.2 %collective-permute-done.3 = f32[4,8,2,48,128]{4,0,3,2,1:T(4,128)} collective-permute-done((f32[4,8,2,48,128]{4,0,3,2,1:T(4,128)S(1)}, f32[4,8,2,48,128]{4,0,3,2,1:T(4,128)}, u32[]{:S(2)}, u32[]{:S(2)}) %collective-permute-start.3) | collective-permute-done | bytes 1572896 | tf_op jit(solution)/shard_map/ppermute | solution.py:36
  152.2 0.0 collective-permute-start.4
  152.2 0.0 copy-done.6
  152.2 0.1 copy.22
  152.3 0.1 copy.24
  152.4 0.1 copy.25
  152.5 0.1 copy.26
  152.7 0.1 copy.27
  152.8 0.1 copy.28
  152.9 0.1 copy.29
  153.0 0.0 copy-done.5
  153.0 0.1 reshape.22
  153.1 0.0 copy-done.4
  153.1 35.6 %collective-permute-done.4 = f32[4,8,2,48,128]{4,0,3,2,1:T(4,128)} collective-permute-done((f32[4,8,2,48,128]{4,0,3,2,1:T(4,128)}, f32[4,8,2,48,128]{4,0,3,2,1:T(4,128)}, u32[]{:S(2)}, u32[]{:S(2)}) %collective-permute-start.4) | collective-permute-done | bytes 1572896 | tf_op jit(solution)/shard_map/ppermute | solution.py:36
  188.6 3.9 %select_add_fusion.1 = (f32[4,8,2,48,128]{4,0,3,2,1:T(4,128)S(1)}, f32[4,8,2,48,128]{4,0,3,2,1:T(4,128)S(1)}) fusion(f32[4,8,2,48,128]{4,0,3,2,1:T(4,128)} %collective-permute-done.4, f32[4,8,2,48,128]{4,0,3,2,1:T(4,128)} %collective-permute-done.3, f32[4,8,2,48,128]{4,0,3,2,1:T(4,128)S(1)} %collective-permute-done.2, pred[4,48]{0,1:T(8,128)(4,1)S(1)} %copy.25, ...), kind=kLoop, calls=%fused_computation.18 | loop fusion | flops 4718592 | bytes 9438528 | tf_op jit(solution)/shard_map/add | solution.py:114
  192.5 0.8 maximum_bitcast_fusion
  193.3 52.7 %copy.30 = f32[4,48,8,2,256]{2,3,1,0,4:T(2,128)} copy(f32[4,48,8,2,256]{4,0,1,3,2:T(4,128)S(1)} %maximum_bitcast_fusion) | data formatting | bytes 6291456 | tf_op jit(solution)/shard_map/vmap(vmap())/transpose | solution.py:99
  246.0 36.2 %gather_fusion = f32[192,8,2,131]{1,2,3,0:T(2,128)} fusion(f32[4,48,8,2,256]{2,3,1,0,4:T(2,128)} %copy.30, s32[192]{0:T(256)S(1)} %reshape.22), kind=kCustom, calls=%fused_computation | custom fusion | bytes 3223296 | tf_op jit(solution)/shard_map/vmap(vmap())/gather | solution.py:99
  282.2 37.2 %copy.31 = f32[4,48,8,2,131]{4,1,3,2,0:T(8,128)S(1)} copy(f32[4,48,8,2,131]{2,3,4,1,0:T(2,128)} %bitcast.24) | data formatting | bytes 3219456 | tf_op jit(solution)/shard_map/vmap(vmap())/gather | solution.py:99
  319.4 0.0 copy-start.1
  319.5 2.5 fusion.2
  (10 shorter events, 0.0 us)
Async XLA Ops:
  6.5 9.1 %copy-start = (f32[8,8]{1,0:T(8,128)S(1)}, f32[8,8]{1,0:T(8,128)}, u32[]{:S(2)}) copy-start(f32[8,8]{1,0:T(8,128)} %param.15) | copy-start | bytes 772
  6.5 8.9 %copy-start.2 = (f32[4,8,2,48,128]{4,3,2,1,0:T(8,128)S(1)}, f32[4,8,2,48,128]{4,3,2,1,0:T(8,128)}, u32[]{:S(2)}) copy-start(f32[4,8,2,48,128]{4,3,2,1,0:T(8,128)} %param.10) | copy-start | bytes 4718596
  6.5 64.0 %all-gather.2.cloned.1.call-start = ((), (), s32[]{:S(2)}) async-start(), calls=%async_computation | async-start | bytes 4718592 | tf_op jit(solution)/shard_map/all_gather | solution.py:150
  9.3 8.8 %collective-permute-start = (f32[4,8,1,48,128]{4,3,2,1,0:T(8,128)}, f32[4,8,1,48,128]{4,3,2,1,0:T(8,128)}, u32[]{:S(2)}, u32[]{:S(2)}) collective-permute-start(f32[4,8,1,48,128]{4,3,2,1,0:T(8,128)} %get-tuple-element.10), channel_id=1, source_target_pairs={{1,0},{3,2},{5,4},{7,6},{9,8},{11,10},{13,12},{15,14},{17,16},{19,... | collective-permute-start | bytes 2359304 | tf_op jit(solution)/shard_map/ppermute | solution.py:29
  10.6 7.5 %collective-permute-start.1 = (f32[4,8,1,48,128]{4,3,2,1,0:T(8,128)}, f32[4,8,1,48,128]{4,3,2,1,0:T(8,128)}, u32[]{:S(2)}, u32[]{:S(2)}) collective-permute-start(f32[4,8,1,48,128]{4,3,2,1,0:T(8,128)} %get-tuple-element.9), channel_id=1, source_target_pairs={{0,1},{2,3},{4,5},{6,7},{8,9},{10,11},{12,13},{14,15},{16,17},{18,... | collective-permute-start | bytes 2359304 | tf_op jit(solution)/shard_map/ppermute | solution.py:28
  18.1 1.5 copy-start.7
  22.7 0.7 copy-start.8
  22.7 0.7 copy-start.9
  22.7 47.8 %copy-start.3 = (f32[8,2,48,128]{3,2,1,0:T(8,128)S(1)}, f32[8,2,48,128]{3,2,1,0:T(8,128)}, u32[]{:S(2)}) copy-start(f32[8,2,48,128]{3,2,1,0:T(8,128)} %param.9) | copy-start | bytes 1179652
  23.8 128.4 %copy-start.6 = (s32[4,48]{1,0:T(4,128)S(1)}, s32[4,48]{1,0:T(4,128)}, u32[]{:S(2)}) copy-start(s32[4,48]{1,0:T(4,128)} %param.12) | copy-start | bytes 2308
  23.8 129.2 %copy-start.5 = (s32[4,48]{1,0:T(4,128)S(1)}, s32[4,48]{1,0:T(4,128)}, u32[]{:S(2)}) copy-start(s32[4,48]{1,0:T(4,128)} %param.13) | copy-start | bytes 2308
  23.8 129.3 %copy-start.4 = (f32[4,48]{1,0:T(4,128)S(1)}, f32[4,48]{1,0:T(4,128)}, u32[]{:S(2)}) copy-start(f32[4,48]{1,0:T(4,128)} %param.14) | copy-start | bytes 2308
  77.0 38.0 %collective-permute-start.2 = (f32[4,8,2,48,128]{4,0,3,2,1:T(4,128)S(1)}, f32[4,8,2,48,128]{4,0,3,2,1:T(4,128)S(1)}, u32[]{:S(2)}, u32[]{:S(2)}) collective-permute-start(f32[4,8,2,48,128]{4,0,3,2,1:T(4,128)S(1)} %multiply_add_fusion), channel_id=1, source_target_pairs={{0,4},{4,8},{8,12},{12,0},{1,5},{5,9},{9,13},{13,1},{2,6},{6,10},{... | collective-permute-start | bytes 4718600 | tf_op jit(solution)/shard_map/ppermute | solution.py:36
  115.0 37.2 %collective-permute-start.3 = (f32[4,8,2,48,128]{4,0,3,2,1:T(4,128)S(1)}, f32[4,8,2,48,128]{4,0,3,2,1:T(4,128)}, u32[]{:S(2)}, u32[]{:S(2)}) collective-permute-start(f32[4,8,2,48,128]{4,0,3,2,1:T(4,128)S(1)} %collective-permute-done.2), channel_id=1, source_target_pairs={{0,4},{4,8},{8,12},{12,0},{1,5},{5,9},{9,13},{13,1},{2,6},{6,10},{... | collective-permute-start | bytes 4718600 | tf_op jit(solution)/shard_map/ppermute | solution.py:36
  152.2 36.5 %collective-permute-start.4 = (f32[4,8,2,48,128]{4,0,3,2,1:T(4,128)}, f32[4,8,2,48,128]{4,0,3,2,1:T(4,128)}, u32[]{:S(2)}, u32[]{:S(2)}) collective-permute-start(f32[4,8,2,48,128]{4,0,3,2,1:T(4,128)} %collective-permute-done.3), channel_id=1, source_target_pairs={{0,4},{4,8},{8,12},{12,0},{1,5},{5,9},{9,13},{13,1},{2,6},{6,10},{... | collective-permute-start | bytes 4718600 | tf_op jit(solution)/shard_map/ppermute | solution.py:36
  319.4 2.6 copy-start.1
Sparse Core Ops, SparseCore 0:
  22.8 47.6 all-gather.1
where the time goes:
time: 330 us; the launch traced here: 329 us
  waiting for transfers between devices  156 us (47%)
  local copies, waits for them, and re-layouts  131 us (40%)
  between operations  13.5 us (4%)
  other arithmetic  11.8 us (4%)
  matrix products  9.28 us (3%)
  starting transfers between devices  7.63 us (2%)
    ppermute x3, waiting for transfers between devices, passed_along(): lax.ppermute(array, axis, [(i, (i + by) % length) for i in range(length)])  109 us
    gather x3, local copies, waits for them, and re-layouts, cut_window(): return lax.dynamic_slice_in_dim(field, start, length, 2)  73.5 us
    transpose x1, local copies, waits for them, and re-layouts, cut_window(): return lax.dynamic_slice_in_dim(field, start, length, 2)  52.7 us
    all_gather x1, waiting for transfers between devices, shards(): lax.all_gather(tendency, 'node', axis=0, tiled=True)  46.7 us
  transfers between devices with their start and end apart: 6, of which 4 were waited for; matrix products, arithmetic and copies ran while one was open for 1% of the time, Pallas kernels for 0%

commit v1 on v0

--- a/solution.py
+++ b/solution.py
@@ -16,6 +16,18 @@
     0.8717401485096066,
     1.0,
 ]
+
+
+def ring_product(x, axis, dim, term):
+    length, mine = (lax.axis_size(axis), lax.axis_index(axis))
+    left = [(i, (i - 1) % length) for i in range(length)]
+    rows = x.shape[dim]
+    carried = x
+    total = term(carried, mine * rows)
+    for hop in range(1, length):
+        carried = lax.ppermute(carried, axis, left)
+        total = total + term(carried, (mine + hop) % length * rows)
+    return total
 
 
 def padded_2(array, sides, width):
@@ -144,11 +156,16 @@
     node_pos = lax.axis_index("node")
     tendency = tendency_of(node_states, reaction_matrix, diffusivity)
     own_rows = lax.dynamic_slice_in_dim(weights, node_pos * slots, slots, 0)
-    integral = jnp.einsum(
-        "mj,jtlyx->mtlyx",
-        own_rows,
-        lax.all_gather(tendency, "node", axis=0, tiled=True),
-        precision=lax.Precision.HIGHEST,
+    integral = ring_product(
+        tendency,
+        "node",
+        0,
+        lambda part, offset: jnp.einsum(
+            "mj,jtlyx->mtlyx",
+            lax.dynamic_slice_in_dim(own_rows, offset, part.shape[0], axis=1),
+            part,
+            precision=lax.Precision.HIGHEST,
+        ),
     )
     sectioned = initial_state[None] + time_step * integral
     return advect_rows(sectioned, sector_depth, cell_offset, fraction)

time: 330 us -> 306 us (0.927)
  waiting for transfers between devices: 156 us -> 139 us
  between operations: 13.5 us -> 0.14 us
  matrix products: 9.28 us -> 14.2 us
  starting transfers between devices: 7.63 us -> 11 us
    all_gather x1 -> x0, waiting for transfers between devices: 46.7 us -> none  [shards(): lax.all_gather(tendency, 'node', axis=0, tiled=True)]
    ppermute x0 -> x1, waiting for transfers between devices: none -> 30.9 us  [ring_product(): carried = lax.ppermute(carried, axis, left)]
    dot_general x1 -> x2, matrix products: 6.51 us -> 9.02 us  [shards(): jnp.einsum('mj,jtlyx->mtlyx', lax.dynamic_slice_in_dim(own_rows, offset,...]
  transfers between devices with their start and end apart: 6 -> 6, of which waited for: 4 -> 4; matrix products, arithmetic and copies ran while one was open for 1% -> 2% of each run, Pallas kernels for 0% -> 0%
where the time goes in v1:
time: 306 us; the launch traced here: 305 us
  waiting for transfers between devices  139 us (45%)
  local copies, waits for them, and re-layouts  132 us (43%)
  matrix products  14.2 us (5%)
  starting transfers between devices  11 us (4%)
  other arithmetic  8.76 us (3%)
    ppermute x3, waiting for transfers between devices, passed_along(): lax.ppermute(array, axis, [(i, (i + by) % length) for i in range(length)])  108 us
    gather x3, local copies, waits for them, and re-layouts, cut_window(): return lax.dynamic_slice_in_dim(field, start, length, 2)  73.5 us
    transpose x1, local copies, waits for them, and re-layouts, cut_window(): return lax.dynamic_slice_in_dim(field, start, length, 2)  52.8 us
    ppermute x1, waiting for transfers between devices, ring_product(): carried = lax.ppermute(carried, axis, left)  30.9 us
    dot_general x2, matrix products, shards(): jnp.einsum('mj,jtlyx->mtlyx', lax.dynamic_slice_in_dim(own_rows, offset,...  9.02 us
  transfers between devices with their start and end apart: 6, of which 4 were waited for; matrix products, arithmetic and copies ran while one was open for 2% of the time, Pallas kernels for 0%

profile of v1, /device:TPU:0, one launch (start us, length us, event | category | flops | bytes accessed | tf_op | source)
XLA Modules:
  0.0 305.3 jit_solution(13050784915487226809)
XLA Ops:
  0.0 0.0 copy-start
  0.0 2.3 copy.12
  2.3 0.0 copy-start.2
  2.4 1.3 fusion.38
  3.6 1.3 collective-permute-start
  4.9 4.8 %collective-permute-start.1 = (f32[4,8,1,48,128]{4,1,3,2,0:T(8,128)}, f32[4,8,1,48,128]{4,1,3,2,0:T(8,128)}, u32[]{:S(2)}, u32[]{:S(2)}) collective-permute-start(f32[4,8,1,48,128]{4,1,3,2,0:T(8,128)} %get-tuple-element.9), channel_id=1, source_target_pairs={{0,1},{2,3},{4,5},{6,7},{8,9},{10,11},{12,13},{14,15},{16,17},{18,... | collective-permute-start | bytes 2359304 | tf_op jit(solution)/shard_map/ppermute | solution.py:40
  9.7 0.0 copy-done.2
  9.7 1.4 tanh.3
  11.1 0.0 collective-permute-done
  11.1 0.0 collective-permute-done.1
  11.1 1.5 broadcast_select_fusion
  12.6 0.0 copy-done
  12.6 0.1 copy-done.3
  12.7 0.0 copy-done.8
  12.7 4.8 %fusion.5 = f32[4,8,2,48,128]{4,1,3,2,0:T(8,128)S(1)} fusion(f32[4,8,1,48,128]{4,1,3,2,0:T(8,128)S(1)} %get-tuple-element.8, f32[4,8,1,48,128]{4,1,3,2,0:T(8,128)} %get-tuple-element.9, f32[4,8,1,48,128]{4,1,3,2,0:T(8,128)} %get-tuple-element.10, f32[4,8,1,48,128]{4,1,3,2,0:T(8,128)S(1)} %get-tuple-element.7, f32[4,8,2,48,128]{4,3,2,1,0:T(8,128)S(1)} %copy-done.3, ...), kind=kOutput, calls=%fused_computation.12 | convolution fusion | flops 40501248 | bytes 7864584 | tf_op jit(solution)/shard_map/ts,mslyx->mtlyx/dot_general | solution.py:104
  17.5 3.0 collective-permute-start.2
  20.5 0.0 copy-done.9
  20.5 0.0 copy-done.10
  20.5 0.2 fusion.16
  20.7 0.2 fusion.15
  20.9 3.6 %fusion.8 = f32[4,8,2,48,128]{4,0,3,2,1:T(4,128)S(1)} fusion(f32[4,8,2,48,128]{4,1,3,2,0:T(8,128)S(1)} %fusion.5, f32[8,8]{1,0:T(8,128)S(1)} %fusion.15, s32[]{:T(128)S(6)} %select_n.58), kind=kOutput, calls=%fused_computation.15 | convolution fusion | flops 18874368 | bytes 3147780 | tf_op jit(solution)/shard_map/mj,jtlyx->mtlyx/dot_general | solution.py:163
  24.4 0.0 copy-start.7
  24.5 0.0 copy-start.6
  24.5 0.0 copy-start.5
  24.5 30.9 %collective-permute-done.2 = f32[4,8,2,48,128]{4,1,3,2,0:T(8,128)} collective-permute-done((f32[4,8,2,48,128]{4,1,3,2,0:T(8,128)S(1)}, f32[4,8,2,48,128]{4,1,3,2,0:T(8,128)}, u32[]{:S(2)}, u32[]{:S(2)}) %collective-permute-start.2) | collective-permute-done | bytes 1572896 | tf_op jit(solution)/shard_map/ppermute | solution.py:28
  55.3 0.0 copy-done.4
  55.3 5.5 %multiply_add_fusion = f32[4,8,2,48,128]{4,0,3,2,1:T(4,128)S(1)} fusion(f32[4,8,2,48,128]{4,0,3,2,1:T(4,128)S(1)} %fusion.8, f32[8,2,48,128]{3,2,1,0:T(8,128)S(1)} %copy-done.4, f32[4,8,2,48,128]{4,1,3,2,0:T(8,128)} %collective-permute-done.2, f32[8,8]{1,0:T(8,128)S(1)} %fusion.15, s32[]{:T(128)S(6)} %select_n.58, s32[]{:T(128)S(6)} %select_n.65), kind=kOutput, calls=%fused_computation.21 | convolution fusion | flops 20054016 | bytes 5113864 | tf_op jit(solution)/shard_map/mj,jtlyx->mtlyx/dot_general | solution.py:163
  60.8 1.9 collective-permute-start.3
  62.7 35.9 %collective-permute-done.3 = f32[4,8,2,48,128]{4,0,3,2,1:T(4,128)S(1)} collective-permute-done((f32[4,8,2,48,128]{4,0,3,2,1:T(4,128)S(1)}, f32[4,8,2,48,128]{4,0,3,2,1:T(4,128)S(1)}, u32[]{:S(2)}, u32[]{:S(2)}) %collective-permute-start.3) | collective-permute-done | bytes 1572896 | tf_op jit(solution)/shard_map/ppermute | solution.py:48
  98.6 0.0 collective-permute-start.4
  98.6 36.9 %collective-permute-done.4 = f32[4,8,2,48,128]{4,0,3,2,1:T(4,128)} collective-permute-done((f32[4,8,2,48,128]{4,0,3,2,1:T(4,128)S(1)}, f32[4,8,2,48,128]{4,0,3,2,1:T(4,128)}, u32[]{:S(2)}, u32[]{:S(2)}) %collective-permute-start.4) | collective-permute-done | bytes 1572896 | tf_op jit(solution)/shard_map/ppermute | solution.py:48
  135.6 0.0 collective-permute-start.5
  135.6 0.1 copy.10
  135.7 0.1 copy.17
  135.8 0.1 copy.18
  135.9 0.1 copy.19
  136.0 0.1 copy.20
  136.1 0.1 copy.21
  136.2 0.1 copy.22
  136.4 0.1 reshape.22
  136.5 35.3 %collective-permute-done.5 = f32[4,8,2,48,128]{4,0,3,2,1:T(4,128)} collective-permute-done((f32[4,8,2,48,128]{4,0,3,2,1:T(4,128)}, f32[4,8,2,48,128]{4,0,3,2,1:T(4,128)}, u32[]{:S(2)}, u32[]{:S(2)}) %collective-permute-start.5) | collective-permute-done | bytes 1572896 | tf_op jit(solution)/shard_map/ppermute | solution.py:48
  171.8 3.9 %select_add_fusion.1 = (f32[4,8,2,48,128]{4,0,3,2,1:T(4,128)S(1)}, f32[4,8,2,48,128]{4,0,3,2,1:T(4,128)S(1)}) fusion(f32[4,8,2,48,128]{4,0,3,2,1:T(4,128)} %collective-permute-done.5, f32[4,8,2,48,128]{4,0,3,2,1:T(4,128)} %collective-permute-done.4, f32[4,8,2,48,128]{4,0,3,2,1:T(4,128)S(1)} %collective-permute-done.3, pred[4,48]{0,1:T(8,128)(4,1)S(1)} %copy.18, ...), kind=kLoop, calls=%fused_computation.20 | loop fusion | flops 4718592 | bytes 9438528 | tf_op jit(solution)/shard_map/add | solution.py:126
  175.7 0.8 maximum_bitcast_fusion
  176.5 52.8 %copy.23 = f32[4,48,8,2,256]{2,3,1,0,4:T(2,128)} copy(f32[4,48,8,2,256]{4,0,1,3,2:T(4,128)S(1)} %maximum_bitcast_fusion) | data formatting | bytes 6291456 | tf_op jit(solution)/shard_map/vmap(vmap())/transpose | solution.py:111
  229.2 36.2 %gather_fusion = f32[192,8,2,131]{1,2,3,0:T(2,128)} fusion(f32[4,48,8,2,256]{2,3,1,0,4:T(2,128)} %copy.23, s32[192]{0:T(256)S(1)} %reshape.22), kind=kCustom, calls=%fused_computation | custom fusion | bytes 3223296 | tf_op jit(solution)/shard_map/vmap(vmap())/gather | solution.py:111
  265.5 37.2 %copy.24 = f32[4,48,8,2,131]{4,1,3,2,0:T(8,128)S(1)} copy(f32[4,48,8,2,131]{2,3,4,1,0:T(2,128)} %bitcast.31) | data formatting | bytes 3219456 | tf_op jit(solution)/shard_map/vmap(vmap())/gather | solution.py:111
  302.7 0.0 copy-start.1
  302.7 2.5 fusion
  (12 shorter events, 0.0 us)
Async XLA Ops:
  0.0 12.6 %copy-start = (f32[8,8]{1,0:T(8,128)S(1)}, f32[8,8]{1,0:T(8,128)}, u32[]{:S(2)}) copy-start(f32[8,8]{1,0:T(8,128)} %param.15) | copy-start | bytes 772
  2.3 7.4 %copy-start.2 = (f32[4,8,2,48,128]{4,3,2,1,0:T(8,128)S(1)}, f32[4,8,2,48,128]{4,3,2,1,0:T(8,128)}, u32[]{:S(2)}) copy-start(f32[4,8,2,48,128]{4,3,2,1,0:T(8,128)} %param.10) | copy-start | bytes 4718596
  3.6 7.4 %collective-permute-start = (f32[4,8,1,48,128]{4,1,3,2,0:T(8,128)}, f32[4,8,1,48,128]{4,1,3,2,0:T(8,128)}, u32[]{:S(2)}, u32[]{:S(2)}) collective-permute-start(f32[4,8,1,48,128]{4,1,3,2,0:T(8,128)} %get-tuple-element.10), channel_id=1, source_target_pairs={{1,0},{3,2},{5,4},{7,6},{9,8},{11,10},{13,12},{15,14},{17,16},{19,... | collective-permute-start | bytes 2359304 | tf_op jit(solution)/shard_map/ppermute | solution.py:41
  4.9 6.2 %collective-permute-start.1 = (f32[4,8,1,48,128]{4,1,3,2,0:T(8,128)}, f32[4,8,1,48,128]{4,1,3,2,0:T(8,128)}, u32[]{:S(2)}, u32[]{:S(2)}) collective-permute-start(f32[4,8,1,48,128]{4,1,3,2,0:T(8,128)} %get-tuple-element.9), channel_id=1, source_target_pairs={{0,1},{2,3},{4,5},{6,7},{8,9},{10,11},{12,13},{14,15},{16,17},{18,... | collective-permute-start | bytes 2359304 | tf_op jit(solution)/shard_map/ppermute | solution.py:40
  11.1 1.6 copy-start.3
  11.1 1.6 copy-start.8
  12.7 7.8 %copy-start.9 = (s32[8]{0:T(128)S(1)}, s32[8]{0:T(128)}, u32[]{:S(2)}) copy-start(s32[8]{0:T(128)} %param.11) | copy-start | bytes 100
  12.7 7.8 %copy-start.10 = (f32[8,8]{1,0:T(8,128)S(1)}, f32[8,8]{1,0:T(8,128)}, u32[]{:S(2)}) copy-start(f32[8,8]{1,0:T(8,128)} %constant.81.clone) | copy-start | bytes 772
  17.5 37.8 %collective-permute-start.2 = (f32[4,8,2,48,128]{4,1,3,2,0:T(8,128)S(1)}, f32[4,8,2,48,128]{4,1,3,2,0:T(8,128)}, u32[]{:S(2)}, u32[]{:S(2)}) collective-permute-start(f32[4,8,2,48,128]{4,1,3,2,0:T(8,128)S(1)} %fusion.5), channel_id=1, source_target_pairs={{0,2},{2,0},{1,3},{3,1},{4,6},{6,4},{5,7},{7,5},{8,10},{10,8},{9,1... | collective-permute-start | bytes 4718600 | tf_op jit(solution)/shard_map/ppermute | solution.py:28
  20.9 34.5 %copy-start.4 = (f32[8,2,48,128]{3,2,1,0:T(8,128)S(1)}, f32[8,2,48,128]{3,2,1,0:T(8,128)}, u32[]{:S(2)}) copy-start(f32[8,2,48,128]{3,2,1,0:T(8,128)} %param.9) | copy-start | bytes 1179652
  24.4 111.1 %copy-start.7 = (s32[4,48]{1,0:T(4,128)S(1)}, s32[4,48]{1,0:T(4,128)}, u32[]{:S(2)}) copy-start(s32[4,48]{1,0:T(4,128)} %param.12) | copy-start | bytes 2308
  24.5 111.9 %copy-start.6 = (s32[4,48]{1,0:T(4,128)S(1)}, s32[4,48]{1,0:T(4,128)}, u32[]{:S(2)}) copy-start(s32[4,48]{1,0:T(4,128)} %param.13) | copy-start | bytes 2308
  24.5 112.0 %copy-start.5 = (f32[4,48]{1,0:T(4,128)S(1)}, f32[4,48]{1,0:T(4,128)}, u32[]{:S(2)}) copy-start(f32[4,48]{1,0:T(4,128)} %param.14) | copy-start | bytes 2308
  60.8 37.8 %collective-permute-start.3 = (f32[4,8,2,48,128]{4,0,3,2,1:T(4,128)S(1)}, f32[4,8,2,48,128]{4,0,3,2,1:T(4,128)S(1)}, u32[]{:S(2)}, u32[]{:S(2)}) collective-permute-start(f32[4,8,2,48,128]{4,0,3,2,1:T(4,128)S(1)} %multiply_add_fusion), channel_id=1, source_target_pairs={{0,4},{4,8},{8,12},{12,0},{1,5},{5,9},{9,13},{13,1},{2,6},{6,10},{... | collective-permute-start | bytes 4718600 | tf_op jit(solution)/shard_map/ppermute | solution.py:48
  98.6 36.9 %collective-permute-start.4 = (f32[4,8,2,48,128]{4,0,3,2,1:T(4,128)S(1)}, f32[4,8,2,48,128]{4,0,3,2,1:T(4,128)}, u32[]{:S(2)}, u32[]{:S(2)}) collective-permute-start(f32[4,8,2,48,128]{4,0,3,2,1:T(4,128)S(1)} %collective-permute-done.3), channel_id=1, source_target_pairs={{0,4},{4,8},{8,12},{12,0},{1,5},{5,9},{9,13},{13,1},{2,6},{6,10},{... | collective-permute-start | bytes 4718600 | tf_op jit(solution)/shard_map/ppermute | solution.py:48
  135.6 36.2 %collective-permute-start.5 = (f32[4,8,2,48,128]{4,0,3,2,1:T(4,128)}, f32[4,8,2,48,128]{4,0,3,2,1:T(4,128)}, u32[]{:S(2)}, u32[]{:S(2)}) collective-permute-start(f32[4,8,2,48,128]{4,0,3,2,1:T(4,128)} %collective-permute-done.4), channel_id=1, source_target_pairs={{0,4},{4,8},{8,12},{12,0},{1,5},{5,9},{9,13},{13,1},{2,6},{6,10},{... | collective-permute-start | bytes 4718600 | tf_op jit(solution)/shard_map/ppermute | solution.py:48
  302.7 2.6 copy-start.1
